TPU v7x, 32 devices: a whole 2x2x4 slice. The times are simulated.
32 devices in a mesh: coil: 2 (over x), ro: 16 (over z, y, core).
Axes of the slice: x: 2, y: 2, z: 4, core: 2. Of those that a mesh axis runs over, the one named last changes fastest.
Arguments:
- kspace: bfloat16 [2, 64, 16, 448, 320], P(None, 'coil', None, 'ro'), may hold values from -884272563206990856199 to 884272563206990856199
- sensitivity: bfloat16 [2, 64, 16, 448, 320], P(None, 'coil', 'ro'), may hold values from -0.75 to 0.75
- sampled: int32 [16, 448], replicated, may hold values 0 or 1
- pole_y: int32 [16, 320], replicated, may hold values from 4 to 112
- order_y: int32 [16, 320], replicated, may hold values from 1 to 3
- pole_z: int32 [16, 448], replicated, may hold values from 4 to 80
- order_z: int32 [16, 448], replicated, may hold values from 1 to 3
Outputs:
- image: float32 [2, 16, 448, 320], P(None, 'ro', 'coil')
All inputs are finite; a program needn't handle non-finite values.
Results may differ from a plain program's by a relative error of at most 0.0056.
Values may be sent and summed in bfloat16 or wider, within the bound.
No kernel may reach another device: no remote copies, remote signals or barrier semaphores. Data moves between devices by JAX's collectives and lax.ppermute only.
A program may use at most 192 MiB of HBM per device.

v0:
```python
import functools
import math

import jax
import jax.numpy as jnp
import ml_dtypes
import numpy as np
from jax import lax
from jax.experimental import pallas as pl
from jax.experimental.pallas import tpu as pltpu
from jax.sharding import PartitionSpec as P

LANES = 128
VMEM_BYTES = 56 * 2**20
FIRST, LATER = (4, 12), (12, 4)
STRAIGHT = (4, 24, 4)
SLOTS = 96


def round_up(value, step):
    return (value + step - 1) // step * step


def dft_tables(length):
    index = np.arange(length, dtype=np.int64)
    product = index[:, None] * index[None, :] % length
    angle = product.astype(np.float32) * np.float32(2.0 * math.pi / length)
    factor = np.float32(1.0 / math.sqrt(length))
    return (
        (np.cos(angle) * factor).astype(ml_dtypes.bfloat16).astype(np.float32),
        (np.sin(angle) * factor).astype(ml_dtypes.bfloat16).astype(np.float32),
    )


def kz_table(length):
    cosine, sine = dft_tables(length)
    table = np.block([[cosine, -sine], [sine, cosine]])
    return jnp.asarray(table.astype(ml_dtypes.bfloat16))


def ky_tables(length, width):
    def padded(part):
        table = np.zeros((length, width), np.float32)
        table[:, :length] = part.T
        return table

    cosine, sine = (padded(part) for part in dft_tables(length))
    table = np.stack([np.concatenate([cosine, sine], axis=1), np.concatenate([-sine, cosine], axis=1)])
    return jnp.asarray(table.astype(ml_dtypes.bfloat16))


def growth(quotient, order):
    square = quotient * quotient
    fourth = square * square
    return 1.0 + jnp.where(order < 1.5, square, jnp.where(order < 2.5, fourth, fourth * square))


def fold(index, length):
    return jnp.minimum(index, length - index).astype(jnp.float32)


def fill_weights(first, sampled_ref, pole_y_ref, order_y_ref, pole_z_ref, order_z_ref, weight):
    lines, readouts, kz_count = weight.shape
    ky_count = sampled_ref.shape[-1]
    width = round_up(lines, LANES)
    line = lax.broadcasted_iota(jnp.int32, (ky_count, width), 1) + first
    place = lax.broadcasted_iota(jnp.int32, (ky_count, width), 0)
    pick = (line == place).astype(jnp.bfloat16)

    def mine(ref):
        return jnp.dot(
            ref[...].astype(jnp.float32).astype(jnp.bfloat16), pick, preferred_element_type=jnp.float32
        )

    sampled, pole_z, order_z = mine(sampled_ref), mine(pole_z_ref), mine(order_z_ref)
    per_y = 1.0 / pole_y_ref[...].astype(jnp.float32)
    per_z = 1.0 / pole_z
    order_y = order_y_ref[...].astype(jnp.float32)
    freq_z = fold(lax.broadcasted_iota(jnp.int32, (readouts, kz_count), 1), kz_count)
    for k in range(lines):
        freq_y = fold(jnp.full((readouts, kz_count), first + k, jnp.int32), ky_count)
        column_y = growth(freq_y * per_y, order_y)
        column_z = growth(freq_z * per_z[:, k : k + 1], order_z[:, k : k + 1])
        weight[k] = sampled[:, k : k + 1] / (column_y * column_z)


def fill_lines(x_ref, weight, packed, coils):
    _, _, lines, readouts, _ = x_ref.shape

    def one(k, _):
        w = weight[k]
        for n, c in enumerate(coils):
            at = pl.ds(pl.multiple_of((n * lines + k) * readouts, 16), readouts)
            line = jnp.concatenate([x_ref[part, c, k].astype(jnp.float32) * w for part in range(2)], axis=1)
            for t in range(packed.shape[0]):
                packed[t, at, :] = line[:, t * LANES : (t + 1) * LANES]
        return 0

    lax.fori_loop(0, lines, one, 0, unroll=4 if lines % 4 == 0 else 2)


def window_kernel(planes, me_ref, x_ref, *refs):
    params, refs = refs[:5], refs[5:]
    outs, (weight, packed) = refs[:-2], refs[-2:]
    _, group, lines, readouts, _ = x_ref.shape

    @pl.when(pl.program_id(0) == 0)
    def _():
        fill_weights(me_ref[1] * lines, *params, weight)

    fill_lines(x_ref, weight, packed, range(group))
    for r in range(readouts):
        k = r % 4 if planes else 0
        readout = r - k + (me_ref[3] ^ k) if planes else r
        o_ref = outs[0].at[r]
        if planes:
            o_ref = outs[k].at[r // 4] if k < 2 else outs[2].at[k - 2, r // 4]
        for t in range(packed.shape[0]):
            o_ref[:, t * LANES : (t + 1) * LANES] = packed[
                t, pl.ds(readout, group * lines, stride=readouts), :
            ].astype(jnp.bfloat16)


def window_chunk(lines_first, me, params, group, planes, start, coils):
    _, _, lines, readouts, kz_count = lines_first.shape
    rows = group * lines
    tail = (coils * lines, 2 * kz_count)
    whole = [pl.BlockSpec(p.shape, lambda i, me: (0, 0)) for p in params]
    heads = [(planes,), (planes,), (2, planes)] if planes else [(readouts,)]
    return pl.pallas_call(
        functools.partial(window_kernel, planes),
        out_shape=[jax.ShapeDtypeStruct((*h, *tail), jnp.bfloat16) for h in heads],
        grid_spec=pltpu.PrefetchScalarGridSpec(
            num_scalar_prefetch=1,
            grid=(coils // group,),
            in_specs=[
                pl.BlockSpec(
                    (2, group, lines, readouts, kz_count), lambda i, me: (0, i + start // group, 0, 0, 0)
                ),
                *whole,
            ],
            out_specs=[
                pl.BlockSpec((*h, rows, tail[1]), lambda i, me, h=h: (*(0 for _ in h), i, 0)) for h in heads
            ],
            scratch_shapes=[
                pltpu.VMEM((lines, readouts, kz_count), jnp.float32),
                pltpu.VMEM((2 * kz_count // LANES, rows * readouts, LANES), jnp.float32),
            ],
        ),
        compiler_params=pltpu.CompilerParams(vmem_limit_bytes=VMEM_BYTES),
        name="window_lines",
    )(me, lines_first, *params)


def one_hot(slots, count):
    row = lax.broadcasted_iota(jnp.int32, (count, slots.shape[-1]), 0).astype(jnp.float32)
    return (row == slots).astype(jnp.bfloat16)


def taken_lines(sampled_ref, first, lines):
    ky_count = sampled_ref.shape[-1]
    place = lax.broadcasted_iota(jnp.int32, (ky_count, LANES), 0)
    lane = lax.broadcasted_iota(jnp.int32, (ky_count, LANES), 1)
    pick = jnp.logical_and(lane + first == place, lane < lines).astype(jnp.bfloat16)
    return jnp.dot(
        sampled_ref[...].astype(jnp.float32).astype(jnp.bfloat16), pick, preferred_element_type=jnp.float32
    )


def source_slots(sampled_ref, source, lines, inner):
    taken = taken_lines(sampled_ref, source * lines, lines)
    readouts = taken.shape[0]
    row = lax.broadcasted_iota(jnp.int32, (LANES, LANES), 0)
    before = (row < lax.broadcasted_iota(jnp.int32, (LANES, LANES), 1)).astype(jnp.bfloat16)
    rank = jnp.dot(taken.astype(jnp.bfloat16), before, preferred_element_type=jnp.float32)
    owner = lax.broadcasted_iota(jnp.int32, (readouts, readouts), 0)
    other = lax.broadcasted_iota(jnp.int32, (readouts, readouts), 1)
    ahead = jnp.logical_and(owner // inner == other // inner, other < owner).astype(jnp.bfloat16)
    past = jnp.dot(ahead, taken.astype(jnp.bfloat16), preferred_element_type=jnp.float32)
    return jnp.where(taken > 0, rank + jnp.sum(past, axis=1, keepdims=True), -1.0)


def among(slots, c, group):
    empty = jnp.full_like(slots, -1.0)
    return [slots if n == c else empty for n in range(group)]


def pack_kernel(by_owner, me_ref, slots_ref, *refs):
    xs, (o_ref, picks) = refs[:-2], refs[-2:]
    outer, group, count, _ = o_ref.shape
    place, plane, within = me_ref[1], me_ref[2], me_ref[3]
    inner, rows = (xs[0].shape[0] // outer, xs[0].shape[1]) if by_owner else (len(xs), xs[0].shape[1])
    lines = rows // group

    @pl.when(pl.program_id(0) == 0)
    def _():
        if by_owner:
            own = source_slots(slots_ref, place, lines, inner)
        for p in range(outer):
            if by_owner:
                slots = [own[p * inner + k : p * inner + k + 1, :lines] for k in range(inner)]
            else:
                slots = [slots_ref[p * inner + within, plane * inner + (within ^ k)] for k in range(inner)]
            for c in range(group):
                picks[p, c] = one_hot(jnp.concatenate(sum([among(s, c, group) for s in slots], []), axis=1), count)

    for p in range(outer):
        blocks = [xs[0][p * inner + k] for k in range(inner)] if by_owner else [x[p] for x in xs]
        held = jnp.concatenate(blocks, axis=0)
        for c in range(group):
            o_ref[p, c] = jnp.dot(picks[p, c], held, preferred_element_type=jnp.float32).astype(jnp.bfloat16)


def block_specs(arrays, rows):
    return [
        pl.BlockSpec((x.shape[0], rows, x.shape[2]), lambda i, me: (0, i, 0))
        if x.ndim == 3
        else pl.BlockSpec((None, x.shape[1], rows, x.shape[3]), lambda i, me: (0, 0, i, 0))
        for x in arrays
    ]


def pack_lines(held, slots, me, outer, inner, lines, count):
    rows_all, packed = held[0].shape[-2:]
    group = inner
    rows = group * lines
    coils = rows_all // lines
    return pl.pallas_call(
        functools.partial(pack_kernel, len(held) == 1),
        out_shape=jax.ShapeDtypeStruct((outer, coils, count, packed), jnp.bfloat16),
        grid_spec=pltpu.PrefetchScalarGridSpec(
            num_scalar_prefetch=1,
            grid=(coils // group,),
            in_specs=[pl.BlockSpec(slots.shape, lambda i, me: (0,) * slots.ndim), *block_specs(held, rows)],
            out_specs=pl.BlockSpec((outer, group, count, packed), lambda i, me: (0, i, 0, 0)),
            scratch_shapes=[pltpu.VMEM((outer, group, count, inner * rows), jnp.bfloat16)],
        ),
        compiler_params=pltpu.CompilerParams(vmem_limit_bytes=VMEM_BYTES),
        name="pack_sampled",
    )(me, slots, *held)


def unpack_kernel(me_ref, sampled_ref, x_ref, own_ref, first_ref, others_ref, places, ranks):
    outer, group, count, packed = x_ref.shape
    inner, rows = places.shape[1], places.shape[2]
    lines = rows // group
    plane, within = me_ref[2], me_ref[3]

    @pl.when(pl.program_id(0) == 0)
    def _():
        for p in range(outer):
            ranks[...] = source_slots(sampled_ref, p * inner + within, lines, inner)
            for k in range(inner):
                slots = ranks[pl.ds(plane * inner + (within ^ k), 1), :][:, :lines]
                row = [jnp.where(slots >= 0, slots + c * count, -1.0) for c in range(group)]
                row = jnp.concatenate([*row, jnp.full((1, -rows % LANES), -1.0, jnp.float32)], axis=1)
                spread = one_hot(row, group * count).astype(jnp.float32).T
                places[p, k] = spread[:rows].astype(jnp.bfloat16)

    for p in range(outer):
        held = x_ref[p].reshape(group * count, packed)
        for k in range(inner):
            out = own_ref.at[p] if k == 0 else first_ref.at[p] if k == 1 else others_ref.at[k - 2, p]
            out[...] = jnp.dot(places[p, k], held, preferred_element_type=jnp.float32).astype(jnp.bfloat16)


def unpack_lines(arrived, sampled, me, inner, lines):
    outer, coils, count, packed = arrived.shape
    group = inner
    rows = group * lines
    tail = (coils * lines, packed)
    heads = [(outer,), (outer,), (2, outer)]
    return pl.pallas_call(
        unpack_kernel,
        out_shape=[jax.ShapeDtypeStruct((*h, *tail), jnp.bfloat16) for h in heads],
        grid_spec=pltpu.PrefetchScalarGridSpec(
            num_scalar_prefetch=1,
            grid=(coils // group,),
            in_specs=[
                pl.BlockSpec(sampled.shape, lambda i, me: (0, 0)),
                pl.BlockSpec((outer, group, count, packed), lambda i, me: (0, i, 0, 0)),
            ],
            out_specs=[
                pl.BlockSpec((*h, rows, packed), lambda i, me, h=h: (*(0 for _ in h), i, 0)) for h in heads
            ],
            scratch_shapes=[
                pltpu.VMEM((outer, inner, rows, group * count), jnp.bfloat16),
                pltpu.VMEM((sampled.shape[0], LANES), jnp.float32),
            ],
        ),
        compiler_params=pltpu.CompilerParams(vmem_limit_bytes=VMEM_BYTES),
        name="unpack_sampled",
    )(me, sampled, arrived)


def most_kernel(inner, outer, sampled_ref, o_ref):
    readouts, ky_count = sampled_ref.shape
    devices = inner * outer
    taken = sampled_ref[...].astype(jnp.float32).astype(jnp.bfloat16)
    line = lax.broadcasted_iota(jnp.int32, (ky_count, LANES), 0)
    lane = lax.broadcasted_iota(jnp.int32, (ky_count, LANES), 1)

    def sums(parts):
        return jnp.dot(
            taken, (line // (ky_count // parts) == lane).astype(jnp.bfloat16), preferred_element_type=jnp.float32
        )

    row = lax.broadcasted_iota(jnp.int32, (readouts, readouts), 0)
    readout = lax.broadcasted_iota(jnp.int32, (readouts, readouts), 1)
    together = (row // inner == readout // inner).astype(jnp.bfloat16)
    by_source = jnp.dot(together, sums(devices).astype(jnp.bfloat16), preferred_element_type=jnp.float32)
    o_ref[0, 0] = jnp.max(jnp.maximum(by_source, sums(outer))).astype(jnp.int32)


def most_lines(sampled, inner, outer):
    return pl.pallas_call(
        functools.partial(most_kernel, inner, outer),
        out_shape=jax.ShapeDtypeStruct((1, 1), jnp.int32),
        out_specs=pl.BlockSpec(memory_space=pltpu.SMEM),
        name="most_lines",
    )(sampled)[0, 0]


def pick_kernel(count, me_ref, slots_ref, table_ref, o_ref):
    o_ref[...] = jnp.zeros_like(o_ref)
    for p in range(slots_ref.shape[1]):
        pick = one_hot(slots_ref[me_ref[1], p], count)
        for part in range(2):
            o_ref[part, pl.ds(p * count, count), :] = jnp.dot(
                pick, table_ref[part, p], preferred_element_type=jnp.float32
            ).astype(jnp.bfloat16)


def pick_rows(table, slots, me, count, depth):
    outer = slots.shape[1]
    table = table.reshape(2, outer, table.shape[1] // outer, table.shape[2])
    shape = (2, depth, table.shape[3])
    return pl.pallas_call(
        functools.partial(pick_kernel, count),
        out_shape=jax.ShapeDtypeStruct(shape, jnp.bfloat16),
        grid_spec=pltpu.PrefetchScalarGridSpec(
            num_scalar_prefetch=1,
            grid=(1,),
            in_specs=[
                pl.BlockSpec(slots.shape, lambda i, me: (0, 0, 0, 0)),
                pl.BlockSpec(table.shape, lambda i, me: (0, 0, 0, 0)),
            ],
            out_specs=pl.BlockSpec(shape, lambda i, me: (0, 0, 0)),
        ),
        compiler_params=pltpu.CompilerParams(vmem_limit_bytes=VMEM_BYTES),
        name="pick_table_rows",
    )(me, slots, table)


def image_kernel(fresh, last, halves, lines, group, pieces, me_ref, *refs):
    xs, refs = refs[:pieces], list(refs[pieces:])
    x_ref, (maps_ref, kz_ref, ky_ref), refs = xs[0], refs[:3], refs[3:]
    acc_in = None if fresh else refs.pop(0)
    outs, (wide, by_line, hybrid, acc) = refs[:-4], refs[-4:]
    kz_count, ky_count = maps_ref.shape[-2:]
    depth = by_line.shape[1]
    width = ky_ref.shape[-1] // 2
    step = pl.program_id(0)

    @pl.when(step == 0)
    def _():
        acc[...] = jnp.zeros_like(acc) if fresh else acc_in[...]
        by_line[...] = jnp.zeros_like(by_line)

    if lines:
        stride = depth // (x_ref.shape[0] * pieces)

        for k in range(pieces):

            def place(s, _, k=k):
                wide[k % 2] = xs[k][s].astype(jnp.float32)
                source = s * pieces + (me_ref[3] ^ k) if pieces > 1 else s
                base = pl.multiple_of(source * stride, stride)
                for c in range(group):
                    by_line[c, pl.ds(base, lines), :] = wide[k % 2, pl.ds(lines * c, lines), :].astype(jnp.bfloat16)
                return 0

            lax.fori_loop(0, x_ref.shape[0], place, 0)
    else:
        count = x_ref.shape[2]
        for c in range(group):
            for p in range(x_ref.shape[0]):
                by_line[c, p * count : (p + 1) * count, :] = x_ref[p, c]

    for c in range(group):
        mixed = lax.dot_general(
            kz_ref[...], by_line[c], (((1,), (1,)), ((), ())), preferred_element_type=jnp.float32
        )
        hybrid[c, :, :depth] = mixed[:kz_count].astype(jnp.bfloat16)
        hybrid[c, :, depth:] = mixed[kz_count:].astype(jnp.bfloat16)
    for c in range(group):
        image = jnp.dot(
            hybrid[c], ky_ref[...].reshape(2 * depth, 2 * width), preferred_element_type=jnp.float32
        )
        real, imag = image[:, :ky_count], image[:, width : width + ky_count]
        map_real = maps_ref[0, c, 0].astype(jnp.float32)
        map_imag = maps_ref[1, c, 0].astype(jnp.float32)
        acc[0] += map_real * real + map_imag * imag
        acc[1] += map_real * imag - map_imag * real

    @pl.when(step == pl.num_programs(0) - 1)
    def _():
        if last and halves == 2:
            keep_ref, send_ref = outs
            rows = ky_count // 2
            lower = me_ref[0] == 0
            for part in range(2):
                low, high = acc[part, :, :rows], acc[part, :, rows:]
                keep_ref[part] = jnp.where(lower, low, high)
                send_ref[part] = jnp.where(lower, high, low).astype(send_ref.dtype)
        else:
            outs[0][...] = acc[...]


def image_chunk(arrived, maps, kz, ky, acc, me, group, lines, start, coils, last, halves):
    kz_count, ky_count = maps.shape[-2:]
    packed = arrived[0].shape[-1]
    depth = ky.shape[1]
    if lines:
        x_specs = block_specs(arrived, group * lines)
    else:
        group = 2
        x_specs = [
            pl.BlockSpec((x.shape[0], group, *x.shape[2:]), lambda i, me: (0, i, 0, 0)) for x in arrived
        ]
    wide = (2, max(group * lines, 8), packed)
    in_specs = [
        *x_specs,
        pl.BlockSpec((2, group, 1, kz_count, ky_count), lambda i, me: (0, i + start // group, 0, 0, 0)),
        pl.BlockSpec(kz.shape, lambda i, me: (0, 0)),
        pl.BlockSpec(ky.shape, lambda i, me: (0, 0, 0)),
    ]
    operands = [*arrived, maps, kz, ky]
    if acc is not None:
        in_specs.append(pl.BlockSpec(acc.shape, lambda i, me: (0, 0, 0)))
        operands.append(acc)
    image_shape = (2, kz_count, ky_count)
    outs = [jax.ShapeDtypeStruct(image_shape, jnp.float32)]
    if last and halves == 2:
        half_shape = (2, kz_count, ky_count // 2)
        outs = [jax.ShapeDtypeStruct(half_shape, jnp.float32), jax.ShapeDtypeStruct(half_shape, jnp.bfloat16)]
    return pl.pallas_call(
        functools.partial(image_kernel, acc is None, last, halves, lines, group, len(arrived)),
        out_shape=outs,
        grid_spec=pltpu.PrefetchScalarGridSpec(
            num_scalar_prefetch=1,
            grid=(coils // group,),
            in_specs=in_specs,
            out_specs=[pl.BlockSpec(o.shape, lambda i, me: (0, 0, 0)) for o in outs],
            scratch_shapes=[
                pltpu.VMEM(wide, jnp.float32),
                pltpu.VMEM((group, depth, packed), jnp.bfloat16),
                pltpu.VMEM((group, kz_count, 2 * depth), jnp.bfloat16),
                pltpu.VMEM(image_shape, jnp.float32),
            ],
        ),
        compiler_params=pltpu.CompilerParams(vmem_limit_bytes=VMEM_BYTES),
        name="image_of_coils",
    )(me, *operands)


def ranks(taken):
    lines = taken.shape[-1]
    before = jnp.asarray(np.triu(np.ones((lines, lines), np.float32), 1).astype(ml_dtypes.bfloat16))
    flat = taken.reshape(-1, lines).astype(jnp.bfloat16)
    rank = jnp.dot(flat, before, preferred_element_type=jnp.float32)
    return jnp.where(flat > 0, rank, -1.0).reshape(taken.shape)


def on_device(kspace, sensitivity, sampled, pole_y, order_y, pole_z, order_z):
    _, coils, readouts, lines, kz_count = kspace.shape
    devices = lax.axis_size("ro")
    halves = lax.axis_size("coil")
    ky_count = lines * devices
    stride = round_up(lines, 16)
    inner = 16 // math.gcd(lines, 16)
    outer = devices // inner
    parts = [(coils,), ()] if inner != 4 or coils != sum(FIRST + LATER) else [FIRST, LATER]
    planned = len(parts[1]) > 0
    place = lax.axis_index("ro")
    me = jnp.stack([lax.axis_index("coil"), place, place // inner, place % inner]).astype(jnp.int32)
    lines_first = jnp.swapaxes(kspace, 2, 3)
    maps = jnp.swapaxes(sensitivity, 3, 4)
    params = (sampled, pole_y, order_y, pole_z, order_z)
    kz = kz_table(kz_count)
    tables = ky_tables(ky_count, round_up(ky_count, LANES))
    ky = jnp.pad(tables.reshape(2, devices, lines, -1), ((0, 0), (0, 0), (0, stride - lines), (0, 0))).reshape(
        2, devices * stride, -1
    )

    def window(planes, start, count):
        return window_chunk(lines_first, me, params, inner, planes, start, count)

    def image(arrived, rows, by_line, start, count, acc, last=False):
        return image_chunk(
            arrived, maps, kz, rows, acc, me, inner, lines if by_line else 0, start, count, last, halves
        )

    def to_place(array, k):
        return lax.ppermute(array, "ro", [(a, a ^ k) for a in range(devices)])

    def in_plane(own, first, others):
        across = to_place(others, 2)
        return [own, to_place(first, 1), across, to_place(across[1], 1)]

    def to_planes(packed):
        same_place = [[p * inner + i for p in range(outer)] for i in range(inner)]
        return lax.all_to_all(
            packed, "ro", split_axis=0, concat_axis=0, tiled=True, axis_index_groups=same_place
        )

    def finish(result):
        if halves == 2:
            keep, give = result
            whole = keep + lax.ppermute(give, "coil", [(0, 1), (1, 0)]).astype(jnp.float32)
        else:
            whole = lax.psum_scatter(result[0], "coil", scatter_dimension=2, tiled=True)
        return jnp.swapaxes(whole, 1, 2)[:, None]

    def straight(first, plan):
        starts = [sum(plan[:i]) for i in range(len(plan))]
        acc, arrived = None, []
        for i, start in enumerate(starts):
            sent = first if i == 0 else window(0, start, plan[i])[0]
            if i >= 2:
                acc = image([arrived[i - 2]], ky, True, starts[i - 2], plan[i - 2], acc)[0]
                sent, acc = lax.optimization_barrier((sent, acc))
            arrived.append(lax.all_to_all(sent, "ro", split_axis=0, concat_axis=0, tiled=True))
        for i in range(max(len(plan) - 2, 0), len(plan)):
            result = image([arrived[i]], ky, True, starts[i], plan[i], acc, i == len(plan) - 1)
            acc = result[0]
        return finish(result)

    if not planned:
        return straight(window(0, 0, coils)[0], (coils,))

    starts = [sum((FIRST + LATER)[:i]) for i in range(len(FIRST + LATER))]
    first_starts, later_starts = starts[: len(FIRST)], starts[len(FIRST) :]

    def pack(held, slots):
        return pack_lines(held, slots, me, outer, inner, lines, SLOTS)

    def spread(part):
        return in_plane(*unpack_lines(part, sampled, me, inner, lines))

    def by_planes(one):
        plane_slots = ranks(sampled.reshape(readouts, outer, inner * lines))
        for_plane = plane_slots.reshape(readouts, devices, 1, lines)
        rows = pick_rows(tables, plane_slots[:, :, None], me, SLOTS, round_up(outer * SLOTS, LANES))
        second = window(0, first_starts[1], FIRST[1])
        later = [window(outer, start, count) for start, count in zip(later_starts, LATER)]
        one = to_planes(one)
        two, one, later[0] = lax.optimization_barrier((pack(second, sampled), one, later[0]))
        two = to_planes(two)
        gathered = [in_plane(*part) for part in later]
        acc = image(spread(one), ky, True, first_starts[0], FIRST[0], None)[0]
        here, acc, rows = lax.optimization_barrier((for_plane, acc, rows))
        three, two = lax.optimization_barrier((pack(gathered[0], here), two))
        three = to_planes(three)
        two = spread(two)
        four, acc, two, three = lax.optimization_barrier((pack(gathered[1], for_plane), acc, two, three))
        four = to_planes(four)
        acc = image(two, ky, True, first_starts[1], FIRST[1], acc)[0]
        acc = image([three], rows, False, later_starts[0], LATER[0], acc)[0]
        return finish(image([four], rows, False, later_starts[1], LATER[1], acc, True))

    first = window(0, 0, FIRST[0])[0]
    return lax.cond(
        most_lines(sampled, inner, outer) <= SLOTS,
        lambda first, packed: by_planes(packed),
        lambda first, packed: straight(first, STRAIGHT),
        first,
        pack([first], sampled),
    )


def solution(mesh):
    return jax.shard_map(
        on_device,
        mesh=mesh,
        in_specs=(
            P(None, "coil", None, "ro", None),
            P(None, "coil", "ro", None, None),
            P(),
            P(),
            P(),
            P(),
            P(),
        ),
        out_specs=P(None, "ro", "coil", None),
        check_vma=False,
    )
```

profile of v0, /device:TPU:14, one launch (start us, length us, event | category | flops | bytes accessed | tf_op | source)
XLA Modules:
  0.0 464.6 jit_solution(2845707232838692711)
XLA Ops:
  0.0 0.1 pad_add_fusion.me_ref
  0.1 1.7 most_lines.1
  2.4 0.0 copy-start.5
  2.5 6.5 %window_lines.11.refs_0_ = bf16[16,112,640]{2,1,0:T(8,128)(2,1)S(1)} custom-call(s32[4]{0:T(128)S(1)} %pad_add_fusion.me_ref, bf16[2,32,28,16,320]{4,3,2,1,0:T(8,128)(2,1)} %bitcast.34, s32[16,448]{1,0:T(8,128)} %slots_ref.1, s32[16,320]{1,0:T(8,128)} %refs_1_.1, s32[16,320]{1,0:T(8,128)} %refs_2_.1, s32[16,448]{1,0:T(8,128)} %refs_3_.1, s32[16,448]{1,0:T(8,128)} %refs_4_.1), custom_call_target="tpu_custom_call" | custom-call | tf_op jit(solution)/shard_map/window_lines/pallas_call | solution.py:130
  8.9 0.0 copy-done.5
  9.0 0.0 copy-start
  9.0 0.0 copy-start.1
  9.0 0.0 copy-start.8
  9.0 0.0 copy-start.9
  9.0 0.0 copy-start.10
  9.0 0.0 copy-start.11
  9.0 3.9 pack_sampled.7
  13.0 0.0 copy-done
  13.0 0.0 copy-done.8
  13.0 450.2 %conditional.1 = (f32[2,1,224,320]{2,3,0,1:T(8,128)S(1)}) conditional(s32[]{:T(128)} %bitcast.11, (s32[4]{0:T(128)S(1)}, bf16[2,32,28,16,320]{4,3,2,1,0:T(8,128)(2,1)}, s32[16,448]{1,0:T(8,128)S(1)}, s32[16,320]{1,0:T(8,128)S(1)}, s32[16,320]{1,0:T(8,128)S(1)}, /*index=5*/s32[16,448]{1,0:T(8,128)S(1)}, s32[16,448]{1,0:T(8,128)S(1)}, ...), branch_computations={%region_0.1_spmd, %region_1.2_spmd} | conditional | flops 1913856 | bytes 174042432 | solution.py:573
  13.0 1.4 copy-done.2
  14.4 6.2 %all-to-all-start = ((bf16[16,112,640]{2,1,0:T(8,128)(2,1)}), bf16[16,112,640]{2,1,0:T(8,128)(2,1)}, u32[]{:S(2)}, u32[]{:S(2)}) async-start(bf16[16,112,640]{2,1,0:T(8,128)(2,1)} %copy-done.2), calls=%async_computation | async-start | bytes 4587520 | tf_op jit(solution)/shard_map/cond/branch_0_fun/all_to_all | solution.py:533
  20.7 25.1 %window_lines.7 = bf16[16,672,640]{2,1,0:T(8,128)(2,1)} custom-call(s32[4]{0:T(128)S(1)} %get-tuple-element.56.me_ref, bf16[2,32,28,16,320]{4,3,2,1,0:T(8,128)(2,1)} %get-tuple-element.57.x_ref, s32[16,448]{1,0:T(8,128)S(1)} %get-tuple-element.58.refs_0_, s32[16,320]{1,0:T(8,128)S(1)} %get-tuple-element.59.refs_1_, s32[16,320]{1,0:T(8,128)S(1)} %get-tuple-element.60.refs_2_, ...), custom_call_target="tpu_custom_call" | custom-call | tf_op jit(solution)/shard_map/cond/branch_0_fun/window_lines/pallas_call | solution.py:130
  45.7 26.5 %all-to-all-done.refs_0_ = bf16[16,112,640]{2,1,0:T(8,128)(2,1)} async-done(((bf16[16,112,640]{2,1,0:T(8,128)(2,1)}), bf16[16,112,640]{2,1,0:T(8,128)(2,1)}, u32[]{:S(2)}, u32[]{:S(2)}) %all-to-all-start) | async-done | bytes 2293792 | tf_op jit(solution)/shard_map/cond/branch_0_fun/all_to_all | solution.py:533
  72.3 5.7 %all-to-all-start.2 = ((bf16[16,672,640]{2,1,0:T(8,128)(2,1)}), bf16[16,672,640]{2,1,0:T(8,128)(2,1)}, u32[]{:S(2)}, u32[]{:S(2)}) async-start(bf16[16,672,640]{2,1,0:T(8,128)(2,1)} %window_lines.7), calls=%async_computation.2 | async-start | bytes 27525120 | tf_op jit(solution)/shard_map/cond/branch_0_fun/all_to_all | solution.py:533
  78.0 7.9 %window_lines.6 = bf16[16,112,640]{2,1,0:T(8,128)(2,1)} custom-call(s32[4]{0:T(128)S(1)} %get-tuple-element.56.me_ref, bf16[2,32,28,16,320]{4,3,2,1,0:T(8,128)(2,1)} %get-tuple-element.57.x_ref, s32[16,448]{1,0:T(8,128)S(1)} %get-tuple-element.58.refs_0_, s32[16,320]{1,0:T(8,128)S(1)} %get-tuple-element.59.refs_1_, s32[16,320]{1,0:T(8,128)S(1)} %get-tuple-element.60.refs_2_, ...), custom_call_target="tpu_custom_call" | custom-call | tf_op jit(solution)/shard_map/cond/branch_0_fun/window_lines/pallas_call | solution.py:130
  85.9 10.5 %image_of_coils.7.refs_4_ = f32[2,320,448]{2,1,0:T(8,128)} custom-call(s32[4]{0:T(128)S(1)} %get-tuple-element.56.me_ref, bf16[16,112,640]{2,1,0:T(8,128)(2,1)} %all-to-all-done.refs_0_, bf16[2,32,1,320,448]{4,3,2,1,0:T(8,128)(2,1)} %get-tuple-element.64.refs_1_, bf16[640,640]{1,0:T(8,128)(2,1)S(1)} %get-tuple-element.65.refs_2_, ...), custom_call_target="tpu_custom_call" | custom-call | tf_op jit(solution)/shard_map/cond/branch_0_fun/image_of_coils/pallas_call | solution.py:447
  96.4 278.8 %all-to-all-done.2.refs_0_ = bf16[16,672,640]{2,1,0:T(8,128)(2,1)} async-done(((bf16[16,672,640]{2,1,0:T(8,128)(2,1)}), bf16[16,672,640]{2,1,0:T(8,128)(2,1)}, u32[]{:S(2)}, u32[]{:S(2)}) %all-to-all-start.2) | async-done | bytes 13762592 | tf_op jit(solution)/shard_map/cond/branch_0_fun/all_to_all | solution.py:533
  375.2 5.4 %all-to-all-start.1 = ((bf16[16,112,640]{2,1,0:T(8,128)(2,1)}), bf16[16,112,640]{2,1,0:T(8,128)(2,1)}, u32[]{:S(2)}, u32[]{:S(2)}) async-start(bf16[16,112,640]{2,1,0:T(8,128)(2,1)} %window_lines.6), calls=%async_computation.1 | async-start | bytes 4587520 | tf_op jit(solution)/shard_map/cond/branch_0_fun/all_to_all | solution.py:533
  380.6 41.7 %image_of_coils.8.refs_4_ = f32[2,320,448]{2,1,0:T(8,128)} custom-call(s32[4]{0:T(128)S(1)} %get-tuple-element.56.me_ref, bf16[16,672,640]{2,1,0:T(8,128)(2,1)} %all-to-all-done.2.refs_0_, bf16[2,32,1,320,448]{4,3,2,1,0:T(8,128)(2,1)} %get-tuple-element.64.refs_1_, bf16[640,640]{1,0:T(8,128)(2,1)S(1)} %get-tuple-element.65.refs_2_, ...), custom_call_target="tpu_custom_call" | custom-call | tf_op jit(solution)/shard_map/cond/branch_0_fun/image_of_coils/pallas_call | solution.py:447
  422.3 9.7 %all-to-all-done.1.refs_0_ = bf16[16,112,640]{2,1,0:T(8,128)(2,1)} async-done(((bf16[16,112,640]{2,1,0:T(8,128)(2,1)}), bf16[16,112,640]{2,1,0:T(8,128)(2,1)}, u32[]{:S(2)}, u32[]{:S(2)}) %all-to-all-start.1) | async-done | bytes 2293792 | tf_op jit(solution)/shard_map/cond/branch_0_fun/all_to_all | solution.py:533
  432.0 11.2 %image_of_coils.9 = (f32[2,320,224]{2,1,0:T(8,128)}, bf16[2,320,224]{2,1,0:T(8,128)(2,1)}) custom-call(s32[4]{0:T(128)S(1)} %get-tuple-element.56.me_ref, bf16[16,112,640]{2,1,0:T(8,128)(2,1)} %all-to-all-done.1.refs_0_, bf16[2,32,1,320,448]{4,3,2,1,0:T(8,128)(2,1)} %get-tuple-element.64.refs_1_, bf16[640,640]{1,0:T(8,128)(2,1)S(1)} %get-tuple-element.65.refs_2_, ...), custom_call_target="tpu_custom_call" | custom-call | tf_op jit(solution)/shard_map/cond/branch_0_fun/image_of_coils/pallas_call | solution.py:447
  443.2 0.5 collective-permute-start
  443.8 9.6 %collective-permute-done = bf16[2,320,224]{2,1,0:T(8,128)(2,1)S(1)} collective-permute-done((bf16[2,320,224]{2,1,0:T(8,128)(2,1)}, bf16[2,320,224]{2,1,0:T(8,128)(2,1)S(1)}, u32[]{:S(2)}, u32[]{:S(2)}) %collective-permute-start) | collective-permute-done | bytes 286752 | tf_op jit(solution)/shard_map/cond/branch_0_fun/ppermute | solution.py:520
  453.4 1.2 add_bitcast_fusion
  463.2 0.0 copy-start.12
  463.2 0.8 copy-done.12
  (5 shorter events, 0.0 us)
Async XLA Ops:
  2.4 6.5 %copy-start.5 = (s32[16,448]{1,0:T(8,128)S(1)}, s32[16,448]{1,0:T(8,128)}, u32[]{:S(2)}) copy-start(s32[16,448]{1,0:T(8,128)} %slots_ref.1) | copy-start | bytes 86020
  9.0 4.0 copy-start
  9.0 4.0 copy-start.1
  9.0 4.0 copy-start.8
  9.0 4.0 copy-start.9
  9.0 4.0 copy-start.10
  9.0 4.0 copy-start.11
  13.0 1.4 copy-start.2
  14.4 57.8 %all-to-all-start = ((bf16[16,112,640]{2,1,0:T(8,128)(2,1)}), bf16[16,112,640]{2,1,0:T(8,128)(2,1)}, u32[]{:S(2)}, u32[]{:S(2)}) async-start(bf16[16,112,640]{2,1,0:T(8,128)(2,1)} %copy-done.2), calls=%async_computation | async-start | bytes 4587520 | tf_op jit(solution)/shard_map/cond/branch_0_fun/all_to_all | solution.py:533
  72.3 302.9 %all-to-all-start.2 = ((bf16[16,672,640]{2,1,0:T(8,128)(2,1)}), bf16[16,672,640]{2,1,0:T(8,128)(2,1)}, u32[]{:S(2)}, u32[]{:S(2)}) async-start(bf16[16,672,640]{2,1,0:T(8,128)(2,1)} %window_lines.7), calls=%async_computation.2 | async-start | bytes 27525120 | tf_op jit(solution)/shard_map/cond/branch_0_fun/all_to_all | solution.py:533
  375.2 56.8 %all-to-all-start.1 = ((bf16[16,112,640]{2,1,0:T(8,128)(2,1)}), bf16[16,112,640]{2,1,0:T(8,128)(2,1)}, u32[]{:S(2)}, u32[]{:S(2)}) async-start(bf16[16,112,640]{2,1,0:T(8,128)(2,1)} %window_lines.6), calls=%async_computation.1 | async-start | bytes 4587520 | tf_op jit(solution)/shard_map/cond/branch_0_fun/all_to_all | solution.py:533
  443.2 10.1 %collective-permute-start = (bf16[2,320,224]{2,1,0:T(8,128)(2,1)}, bf16[2,320,224]{2,1,0:T(8,128)(2,1)S(1)}, u32[]{:S(2)}, u32[]{:S(2)}) collective-permute-start(bf16[2,320,224]{2,1,0:T(8,128)(2,1)} %get-tuple-element.70), channel_id=1, source_target_pairs={{0,16},{16,0},{1,17},{17,1},{2,18},{18,2},{3,19},{19,3},{4,20},{20... | collective-permute-start | bytes 860168 | tf_op jit(solution)/shard_map/cond/branch_0_fun/ppermute | solution.py:520
  463.2 0.8 copy-start.12
where the time goes:
time: 471 us; the launch traced here: 465 us
  waiting for transfers between devices  325 us (69%)
  Pallas kernels  109 us (23%)
  starting transfers between devices  17.9 us (4%)
  loops' own time  8.75 us (2%)
    all_to_all x3, waiting for transfers between devices, straight(): lax.all_to_all(sent, 'ro', split_axis=0, concat_axis=0, tiled=True)  315 us
    pallas_call x3, Pallas kernels, image_chunk(): pl.pallas_call(functools.partial(image_kernel, acc is None, last, halves,...  63.5 us
    pallas_call x3, Pallas kernels, window_chunk(): pl.pallas_call(functools.partial(window_kernel, planes), out_shape=[jax.S...  39.4 us
    all_to_all x3, starting transfers between devices, straight(): lax.all_to_all(sent, 'ro', split_axis=0, concat_axis=0, tiled=True)  17.3 us
    ppermute x1, waiting for transfers between devices, finish(): lax.ppermute(give, 'coil', [(0, 1), (1, 0)]).astype(jnp.float32)  9.6 us
  transfers between devices with their start and end apart: 4, of which 4 were waited for; matrix products, arithmetic and copies ran while one was open for 0% of the time, Pallas kernels for 18%

commit v1 on v0

--- a/solution.py
+++ b/solution.py
@@ -312,13 +312,39 @@
     o_ref[0, 0] = jnp.max(jnp.maximum(by_source, sums(outer))).astype(jnp.int32)
 
 
-def most_lines(sampled, inner, outer):
-    return pl.pallas_call(
-        functools.partial(most_kernel, inner, outer),
-        out_shape=jax.ShapeDtypeStruct((1, 1), jnp.int32),
-        out_specs=pl.BlockSpec(memory_space=pltpu.SMEM),
-        name="most_lines",
-    )(sampled)[0, 0]
+def first_kernel(inner, outer, me_ref, x_ref, *refs):
+    params, (o_ref, packed_ref, most_ref, weight, tiles, picks) = refs[:5], refs[5:]
+    window_kernel(0, me_ref, x_ref, *params, o_ref, weight, tiles)
+    pack_kernel(True, me_ref, params[0], o_ref, packed_ref, picks)
+    most_kernel(inner, outer, params[0], most_ref)
+
+
+def first_chunk(lines_first, me, params, inner, outer, count):
+    _, _, lines, readouts, kz_count = lines_first.shape
+    rows, packed = inner * lines, 2 * kz_count
+    shapes = [(readouts, rows, packed), (outer, inner, count, packed)]
+    whole = [pl.BlockSpec(p.shape, lambda i, me: (0, 0)) for p in params]
+    *arrays, most = pl.pallas_call(
+        functools.partial(first_kernel, inner, outer),
+        out_shape=[*(jax.ShapeDtypeStruct(s, jnp.bfloat16) for s in shapes), jax.ShapeDtypeStruct((1, 1), jnp.int32)],
+        grid_spec=pltpu.PrefetchScalarGridSpec(
+            num_scalar_prefetch=1,
+            grid=(1,),
+            in_specs=[pl.BlockSpec((2, inner, lines, readouts, kz_count), lambda i, me: (0, 0, 0, 0, 0)), *whole],
+            out_specs=[
+                *(pl.BlockSpec(s, lambda i, me, n=len(s): (0,) * n) for s in shapes),
+                pl.BlockSpec(memory_space=pltpu.SMEM),
+            ],
+            scratch_shapes=[
+                pltpu.VMEM((lines, readouts, kz_count), jnp.float32),
+                pltpu.VMEM((packed // LANES, rows * readouts, LANES), jnp.float32),
+                pltpu.VMEM((outer, inner, count, inner * rows), jnp.bfloat16),
+            ],
+        ),
+        compiler_params=pltpu.CompilerParams(vmem_limit_bytes=VMEM_BYTES),
+        name="window_and_pack",
+    )(me, lines_first, *params)
+    return *arrays, most[0, 0]
 
 
 def pick_kernel(count, me_ref, slots_ref, table_ref, o_ref):
@@ -424,7 +450,7 @@
     if lines:
         x_specs = block_specs(arrived, group * lines)
     else:
-        group = 2
+        group = 2 if last else group
         x_specs = [
             pl.BlockSpec((x.shape[0], group, *x.shape[2:]), lambda i, me: (0, i, 0, 0)) for x in arrived
         ]
@@ -481,7 +507,7 @@
     inner = 16 // math.gcd(lines, 16)
     outer = devices // inner
     parts = [(coils,), ()] if inner != 4 or coils != sum(FIRST + LATER) else [FIRST, LATER]
-    planned = len(parts[1]) > 0
+    planned = len(parts[1]) > 0 and FIRST[0] == STRAIGHT[0] == inner
     place = lax.axis_index("ro")
     me = jnp.stack([lax.axis_index("coil"), place, place // inner, place % inner]).astype(jnp.int32)
     lines_first = jnp.swapaxes(kspace, 2, 3)
@@ -553,29 +579,32 @@
         for_plane = plane_slots.reshape(readouts, devices, 1, lines)
         rows = pick_rows(tables, plane_slots[:, :, None], me, SLOTS, round_up(outer * SLOTS, LANES))
         second = window(0, first_starts[1], FIRST[1])
-        later = [window(outer, start, count) for start, count in zip(later_starts, LATER)]
+        third = window(outer, later_starts[0], LATER[0])
         one = to_planes(one)
-        two, one, later[0] = lax.optimization_barrier((pack(second, sampled), one, later[0]))
+        two, one, third = lax.optimization_barrier((pack(second, sampled), one, third))
         two = to_planes(two)
-        gathered = [in_plane(*part) for part in later]
-        acc = image(spread(one), ky, True, first_starts[0], FIRST[0], None)[0]
-        here, acc, rows = lax.optimization_barrier((for_plane, acc, rows))
-        three, two = lax.optimization_barrier((pack(gathered[0], here), two))
+        third = in_plane(*third)
+        one = spread(one)
+        here, one, rows = lax.optimization_barrier((for_plane, one, rows))
+        three, two = lax.optimization_barrier((pack(third, here), two))
         three = to_planes(three)
+        acc = image(one, ky, True, first_starts[0], FIRST[0], None)[0]
+        after, acc = lax.optimization_barrier((me, acc))
         two = spread(two)
-        four, acc, two, three = lax.optimization_barrier((pack(gathered[1], for_plane), acc, two, three))
+        fourth = in_plane(*window_chunk(lines_first, after, params, inner, outer, later_starts[1], LATER[1]))
+        four, acc, two, three = lax.optimization_barrier((pack(fourth, for_plane), acc, two, three))
         four = to_planes(four)
         acc = image(two, ky, True, first_starts[1], FIRST[1], acc)[0]
         acc = image([three], rows, False, later_starts[0], LATER[0], acc)[0]
         return finish(image([four], rows, False, later_starts[1], LATER[1], acc, True))
 
-    first = window(0, 0, FIRST[0])[0]
+    first, packed, most = first_chunk(lines_first, me, params, inner, outer, SLOTS)
     return lax.cond(
-        most_lines(sampled, inner, outer) <= SLOTS,
+        most <= SLOTS,
         lambda first, packed: by_planes(packed),
         lambda first, packed: straight(first, STRAIGHT),
         first,
-        pack([first], sampled),
+        packed,
     )
 
 

time: 471 us -> 416 us (0.88)
  the two profiles are of different devices: /device:TPU:14 before, /device:TPU:0 now
where the time goes in v1:
time: 416 us; the launch traced here: 410 us
  waiting for transfers between devices  208 us (50%)
  Pallas kernels  157 us (38%)
  starting transfers between devices  28.4 us (7%)
  loops' own time  6.99 us (2%)
  local copies, waits for them, and re-layouts  6.08 us (1%)
    ppermute x12, waiting for transfers between devices, to_place(): return lax.ppermute(array, 'ro', [(a, a ^ k) for a in range(devices)])  170 us
    pallas_call x4, Pallas kernels, image_chunk(): pl.pallas_call(functools.partial(image_kernel, acc is None, last, halves,...  63.7 us
    pallas_call x3, Pallas kernels, window_chunk(): pl.pallas_call(functools.partial(window_kernel, planes), out_shape=[jax.S...  38 us
    all_to_all x4, waiting for transfers between devices, to_planes(): lax.all_to_all(packed, 'ro', split_axis=0, concat_axis=0, tiled=True, axi...  31.3 us
    pallas_call x3, Pallas kernels, pack_lines(): pl.pallas_call(functools.partial(pack_kernel, len(held) == 1), out_shape=...  24.8 us
    all_to_all x4, starting transfers between devices, to_planes(): lax.all_to_all(packed, 'ro', split_axis=0, concat_axis=0, tiled=True, axi...  21.7 us
    pallas_call x2, Pallas kernels, unpack_lines(): pl.pallas_call(unpack_kernel, out_shape=[jax.ShapeDtypeStruct((*h, *tail)...  16.8 us
    pallas_call x1, Pallas kernels, first_chunk(): pl.pallas_call(functools.partial(first_kernel, inner, outer), out_shape=[...  10.1 us
  transfers between devices with their start and end apart: 17, of which 10 were waited for; matrix products, arithmetic and copies ran while one was open for 1% of the time, Pallas kernels for 34%

profile of v1, /device:TPU:0, one launch (start us, length us, event | category | flops | bytes accessed | tf_op | source)
XLA Modules:
  0.0 409.5 jit_solution(15827524638380471260)
XLA Ops:
  0.1 10.1 %window_and_pack.1 = (bf16[16,112,640]{2,1,0:T(8,128)(2,1)}, bf16[4,4,96,640]{3,2,1,0:T(8,128)(2,1)}, s32[1,1]{1,0:T(1,128)}) custom-call(s32[4]{0:T(128)S(1)} %pad_add_fusion.me_ref, bf16[2,32,28,16,320]{4,3,2,1,0:T(8,128)(2,1)} %bitcast.34, s32[16,448]{1,0:T(8,128)} %refs_0_.1, s32[16,320]{1,0:T(8,128)} %refs_1_.1, s32[16,320]{1,0:T(8,128)} %refs_2_.1, ...), custom_call_target="tpu_custom_call" | custom-call | tf_op jit(solution)/shard_map/window_and_pack/pallas_call | solution.py:327
  10.9 397.5 %conditional.1 = (f32[2,1,224,320]{2,3,0,1:T(8,128)S(1)}) conditional(s32[]{:T(128)} %bitcast.16, (s32[4]{0:T(128)S(1)}, bf16[2,32,28,16,320]{4,3,2,1,0:T(8,128)(2,1)}, s32[16,448]{1,0:T(8,128)S(1)}, s32[16,320]{1,0:T(8,128)S(1)}, s32[16,320]{1,0:T(8,128)S(1)}, /*index=5*/s32[16,448]{1,0:T(8,128)S(1)}, s32[16,448]{1,0:T(8,128)S(1)}, ...), branch_computations={%region_0.1_spmd, %region_1.2_spmd} | conditional | flops 1913856 | bytes 174042432 | solution.py:602
  17.5 6.3 %all-to-all-start.3 = ((bf16[4,4,96,640]{3,2,1,0:T(8,128)(2,1)}), bf16[4,4,96,640]{3,2,1,0:T(8,128)(2,1)}, u32[]{:S(2)}, u32[]{:S(2)}) async-start(bf16[4,4,96,640]{3,2,1,0:T(8,128)(2,1)} %get-tuple-element.79), calls=%async_computation.3 | async-start | bytes 3932160 | tf_op jit(solution)/shard_map/cond/branch_1_fun/all_to_all | solution.py:539
  23.9 14.7 %window_lines.7.refs_0_ = bf16[16,336,640]{2,1,0:T(8,128)(2,1)} custom-call(s32[4]{0:T(128)S(1)} %get-tuple-element.95.me_ref, bf16[2,32,28,16,320]{4,3,2,1,0:T(8,128)(2,1)} %get-tuple-element.74.x_ref, s32[16,448]{1,0:T(8,128)S(1)} %get-tuple-element.72.refs_0_.slots_ref.sampled_ref, s32[16,320]{1,0:T(8,128)S(1)} %get-tuple-element.75.refs_1_, ...), custom_call_target="tpu_custom_call" | custom-call | tf_op jit(solution)/shard_map/cond/branch_1_fun/window_lines/pallas_call | solution.py:130
  38.6 15.2 %window_lines.8 = (bf16[4,336,640]{2,1,0:T(8,128)(2,1)}, bf16[4,336,640]{2,1,0:T(8,128)(2,1)}, bf16[2,4,336,640]{3,2,1,0:T(8,128)(2,1)}) custom-call(s32[4]{0:T(128)S(1)} %get-tuple-element.95.me_ref, bf16[2,32,28,16,320]{4,3,2,1,0:T(8,128)(2,1)} %get-tuple-element.74.x_ref, s32[16,448]{1,0:T(8,128)S(1)} %get-tuple-element.72.refs_0_.slots_ref.sampled_ref, ...), custom_call_target="tpu_custom_call" | custom-call | tf_op jit(solution)/shard_map/cond/branch_1_fun/window_lines/pallas_call | solution.py:130
  53.7 10.0 %pack_sampled.3 = bf16[4,12,96,640]{3,2,1,0:T(8,128)(2,1)} custom-call(s32[4]{0:T(128)S(1)} %get-tuple-element.95.me_ref, s32[16,448]{1,0:T(8,128)S(1)} %get-tuple-element.72.refs_0_.slots_ref.sampled_ref, bf16[16,336,640]{2,1,0:T(8,128)(2,1)} %window_lines.7.refs_0_), custom_call_target="tpu_custom_call" | custom-call | tf_op jit(solution)/shard_map/cond/branch_1_fun/pack_sampled/pallas_call | solution.py:228
  63.8 5.6 %all-to-all-done.3.x_ref = bf16[4,4,96,640]{3,2,1,0:T(8,128)(2,1)} async-done(((bf16[4,4,96,640]{3,2,1,0:T(8,128)(2,1)}), bf16[4,4,96,640]{3,2,1,0:T(8,128)(2,1)}, u32[]{:S(2)}, u32[]{:S(2)}) %all-to-all-start.3) | async-done | bytes 1966112 | tf_op jit(solution)/shard_map/cond/branch_1_fun/all_to_all | solution.py:539
  69.3 5.6 %all-to-all-start.4 = ((bf16[4,12,96,640]{3,2,1,0:T(8,128)(2,1)}), bf16[4,12,96,640]{3,2,1,0:T(8,128)(2,1)}, u32[]{:S(2)}, u32[]{:S(2)}) async-start(bf16[4,12,96,640]{3,2,1,0:T(8,128)(2,1)} %pack_sampled.3), calls=%async_computation.4 | async-start | bytes 11796480 | tf_op jit(solution)/shard_map/cond/branch_1_fun/all_to_all | solution.py:539
  75.0 1.6 collective-permute-start.8
  76.6 6.0 %unpack_sampled.2 = (bf16[4,112,640]{2,1,0:T(8,128)(2,1)}, bf16[4,112,640]{2,1,0:T(8,128)(2,1)}, bf16[2,4,112,640]{3,2,1,0:T(8,128)(2,1)}) custom-call(s32[4]{0:T(128)S(1)} %get-tuple-element.95.me_ref, s32[16,448]{1,0:T(8,128)S(1)} %get-tuple-element.72.refs_0_.slots_ref.sampled_ref, bf16[4,4,96,640]{3,2,1,0:T(8,128)(2,1)} %all-to-all-done.3.x_ref), custom_call_target="tpu_custom_call" | custom-call | tf_op jit(solution)/shard_map/cond/branch_1_fun/unpack_sampled/pallas_call | solution.py:273
  83.1 69.5 %collective-permute-done.8.refs_2_ = bf16[2,4,336,640]{3,2,1,0:T(8,128)(2,1)S(1)} collective-permute-done((bf16[2,4,336,640]{3,2,1,0:T(8,128)(2,1)}, bf16[2,4,336,640]{3,2,1,0:T(8,128)(2,1)S(1)}, u32[]{:S(2)}, u32[]{:S(2)}) %collective-permute-start.8) | collective-permute-done | bytes 3440672 | tf_op jit(solution)/shard_map/cond/branch_1_fun/ppermute | solution.py:531
  154.6 20.6 %collective-permute-done.2.refs_2_ = bf16[2,4,112,640]{3,2,1,0:T(8,128)(2,1)S(1)} collective-permute-done((bf16[2,4,112,640]{3,2,1,0:T(8,128)(2,1)}, bf16[2,4,112,640]{3,2,1,0:T(8,128)(2,1)S(1)}, u32[]{:S(2)}, u32[]{:S(2)}) %collective-permute-start.2) | collective-permute-done | bytes 1146912 | tf_op jit(solution)/shard_map/cond/branch_1_fun/ppermute | solution.py:531
  177.6 3.8 pick_table_rows.1.refs_3_
  181.4 9.6 %pack_sampled.5 = bf16[4,12,96,640]{3,2,1,0:T(8,128)(2,1)} custom-call(s32[4]{0:T(128)S(1)} %get-tuple-element.95.me_ref, f32[16,16,1,28]{3,2,1,0:T(1,128)} %reshape.16.slots_ref, bf16[4,336,640]{2,1,0:T(8,128)(2,1)} %get-tuple-element.101.refs_0_, bf16[4,336,640]{2,1,0:T(8,128)(2,1)} %collective-permute-done.7.refs_1_, bf16[2,4,336,640]{3,2,1,0:T(8,128)(2,1)} %copy-done.3, ...), custom_call_target="tpu_custom_call" | custom-call | tf_op jit(solution)/shard_map/cond/branch_1_fun/pack_sampled/pallas_call | solution.py:228
  191.1 13.1 %all-to-all-done.4.x_ref = bf16[4,12,96,640]{3,2,1,0:T(8,128)(2,1)} async-done(((bf16[4,12,96,640]{3,2,1,0:T(8,128)(2,1)}), bf16[4,12,96,640]{3,2,1,0:T(8,128)(2,1)}, u32[]{:S(2)}, u32[]{:S(2)}) %all-to-all-start.4) | async-done | bytes 5898272 | tf_op jit(solution)/shard_map/cond/branch_1_fun/all_to_all | solution.py:539
  204.2 5.3 %all-to-all-start.5 = ((bf16[4,12,96,640]{3,2,1,0:T(8,128)(2,1)}), bf16[4,12,96,640]{3,2,1,0:T(8,128)(2,1)}, u32[]{:S(2)}, u32[]{:S(2)}) async-start(bf16[4,12,96,640]{3,2,1,0:T(8,128)(2,1)} %pack_sampled.5), calls=%async_computation.5 | async-start | bytes 11796480 | tf_op jit(solution)/shard_map/cond/branch_1_fun/all_to_all | solution.py:539
  209.5 10.8 %unpack_sampled.3 = (bf16[4,336,640]{2,1,0:T(8,128)(2,1)}, bf16[4,336,640]{2,1,0:T(8,128)(2,1)}, bf16[2,4,336,640]{3,2,1,0:T(8,128)(2,1)}) custom-call(s32[4]{0:T(128)S(1)} %get-tuple-element.95.me_ref, s32[16,448]{1,0:T(8,128)S(1)} %get-tuple-element.72.refs_0_.slots_ref.sampled_ref, bf16[4,12,96,640]{3,2,1,0:T(8,128)(2,1)} %all-to-all-done.4.x_ref), custom_call_target="tpu_custom_call" | custom-call | tf_op jit(solution)/shard_map/cond/branch_1_fun/unpack_sampled/pallas_call | solution.py:273
  220.3 1.5 collective-permute-start.11
  221.9 10.6 %image_of_coils.10.refs_7_ = f32[2,320,448]{2,1,0:T(8,128)} custom-call(s32[4]{0:T(128)S(1)} %get-tuple-element.95.me_ref, bf16[4,112,640]{2,1,0:T(8,128)(2,1)} %get-tuple-element.88.refs_0_, bf16[4,112,640]{2,1,0:T(8,128)(2,1)} %collective-permute-done.1.refs_1_, bf16[2,4,112,640]{3,2,1,0:T(8,128)(2,1)} %copy-done.6, ...), custom_call_target="tpu_custom_call" | custom-call | tf_op jit(solution)/shard_map/cond/branch_1_fun/image_of_coils/pallas_call | solution.py:473
  232.5 8.1 %window_lines.9 = (bf16[4,112,640]{2,1,0:T(8,128)(2,1)}, bf16[4,112,640]{2,1,0:T(8,128)(2,1)}, bf16[2,4,112,640]{3,2,1,0:T(8,128)(2,1)}) custom-call(s32[4]{0:T(128)S(1)} %get-tuple-element.95.me_ref, bf16[2,32,28,16,320]{4,3,2,1,0:T(8,128)(2,1)} %get-tuple-element.74.x_ref, s32[16,448]{1,0:T(8,128)S(1)} %get-tuple-element.72.refs_0_.slots_ref.sampled_ref, ...), custom_call_target="tpu_custom_call" | custom-call | tf_op jit(solution)/shard_map/cond/branch_1_fun/window_lines/pallas_call | solution.py:130
  241.1 56.8 %collective-permute-done.11.refs_2_ = bf16[2,4,336,640]{3,2,1,0:T(8,128)(2,1)S(1)} collective-permute-done((bf16[2,4,336,640]{3,2,1,0:T(8,128)(2,1)}, bf16[2,4,336,640]{3,2,1,0:T(8,128)(2,1)S(1)}, u32[]{:S(2)}, u32[]{:S(2)}) %collective-permute-start.11) | collective-permute-done | bytes 3440672 | tf_op jit(solution)/shard_map/cond/branch_1_fun/ppermute | solution.py:531
  299.9 20.6 %collective-permute-done.5.refs_2_ = bf16[2,4,112,640]{3,2,1,0:T(8,128)(2,1)S(1)} collective-permute-done((bf16[2,4,112,640]{3,2,1,0:T(8,128)(2,1)}, bf16[2,4,112,640]{3,2,1,0:T(8,128)(2,1)S(1)}, u32[]{:S(2)}, u32[]{:S(2)}) %collective-permute-start.5) | collective-permute-done | bytes 1146912 | tf_op jit(solution)/shard_map/cond/branch_1_fun/ppermute | solution.py:531
  320.7 2.1 collective-permute-done.6.refs_3_
  322.8 5.2 %pack_sampled.4 = bf16[4,4,96,640]{3,2,1,0:T(8,128)(2,1)} custom-call(s32[4]{0:T(128)S(1)} %get-tuple-element.95.me_ref, f32[16,16,1,28]{3,2,1,0:T(1,128)} %reshape.16.slots_ref, bf16[4,112,640]{2,1,0:T(8,128)(2,1)} %get-tuple-element.96.refs_0_, bf16[4,112,640]{2,1,0:T(8,128)(2,1)} %copy-done.12, bf16[2,4,112,640]{3,2,1,0:T(8,128)(2,1)} %copy-done.5, ...), custom_call_target="tpu_custom_call" | custom-call | tf_op jit(solution)/shard_map/cond/branch_1_fun/pack_sampled/pallas_call | solution.py:228
  327.9 10.8 %all-to-all-done.5.refs_0_ = bf16[4,12,96,640]{3,2,1,0:T(8,128)(2,1)} async-done(((bf16[4,12,96,640]{3,2,1,0:T(8,128)(2,1)}), bf16[4,12,96,640]{3,2,1,0:T(8,128)(2,1)}, u32[]{:S(2)}, u32[]{:S(2)}) %all-to-all-start.5) | async-done | bytes 5898272 | tf_op jit(solution)/shard_map/cond/branch_1_fun/all_to_all | solution.py:539
  338.8 4.4 %all-to-all-start.6 = ((bf16[4,4,96,640]{3,2,1,0:T(8,128)(2,1)}), bf16[4,4,96,640]{3,2,1,0:T(8,128)(2,1)}, u32[]{:S(2)}, u32[]{:S(2)}) async-start(bf16[4,4,96,640]{3,2,1,0:T(8,128)(2,1)} %pack_sampled.4), calls=%async_computation.6 | async-start | bytes 3932160 | tf_op jit(solution)/shard_map/cond/branch_1_fun/all_to_all | solution.py:539
  343.2 23.4 %image_of_coils.11.refs_4_ = f32[2,320,448]{2,1,0:T(8,128)} custom-call(s32[4]{0:T(128)S(1)} %get-tuple-element.95.me_ref, bf16[4,336,640]{2,1,0:T(8,128)(2,1)} %get-tuple-element.113.refs_0_, bf16[4,336,640]{2,1,0:T(8,128)(2,1)} %collective-permute-done.10.refs_1_, bf16[2,4,336,640]{3,2,1,0:T(8,128)(2,1)} %copy-done.2, ...), custom_call_target="tpu_custom_call" | custom-call | tf_op jit(solution)/shard_map/cond/branch_1_fun/image_of_coils/pallas_call | solution.py:473
  366.5 19.8 %image_of_coils.12.refs_4_ = f32[2,320,448]{2,1,0:T(8,128)} custom-call(s32[4]{0:T(128)S(1)} %get-tuple-element.95.me_ref, bf16[4,12,96,640]{3,2,1,0:T(8,128)(2,1)} %all-to-all-done.5.refs_0_, bf16[2,32,1,320,448]{4,3,2,1,0:T(8,128)(2,1)} %get-tuple-element.92.refs_4_.refs_1_, bf16[640,640]{1,0:T(8,128)(2,1)S(1)} %get-tuple-element.93.refs_5_.refs_2_, ...), custom_call_target="tpu_custom_call" | custom-call | tf_op jit(solution)/shard_map/cond/branch_1_fun/image_of_coils/pallas_call | solution.py:473
  386.3 1.8 all-to-all-done.6.refs_0_
  388.1 9.9 %image_of_coils.13 = (f32[2,320,224]{2,1,0:T(8,128)}, bf16[2,320,224]{2,1,0:T(8,128)(2,1)}) custom-call(s32[4]{0:T(128)S(1)} %get-tuple-element.95.me_ref, bf16[4,4,96,640]{3,2,1,0:T(8,128)(2,1)} %all-to-all-done.6.refs_0_, bf16[2,32,1,320,448]{4,3,2,1,0:T(8,128)(2,1)} %get-tuple-element.92.refs_4_.refs_1_, ...), custom_call_target="tpu_custom_call" | custom-call | tf_op jit(solution)/shard_map/cond/branch_1_fun/image_of_coils/pallas_call | solution.py:473
  398.1 1.5 collective-permute-start.13
  399.6 7.4 %collective-permute-done.13 = bf16[2,320,224]{2,1,0:T(8,128)(2,1)S(1)} collective-permute-done((bf16[2,320,224]{2,1,0:T(8,128)(2,1)}, bf16[2,320,224]{2,1,0:T(8,128)(2,1)S(1)}, u32[]{:S(2)}, u32[]{:S(2)}) %collective-permute-start.13) | collective-permute-done | bytes 286752 | tf_op jit(solution)/shard_map/cond/branch_1_fun/ppermute | solution.py:546
  (59 shorter events, 9.6 us)
Async XLA Ops:
  0.1 10.8 %copy-start = (bf16[2,512,1024]{2,1,0:T(8,128)(2,1)S(1)}, bf16[2,512,1024]{2,1,0:T(8,128)(2,1)}, u32[]{:S(2)}) copy-start(bf16[2,512,1024]{2,1,0:T(8,128)(2,1)} %constant.60) | copy-start | bytes 6291460
  0.1 10.8 %copy-start.1 = (bf16[640,640]{1,0:T(8,128)(2,1)S(1)}, bf16[640,640]{1,0:T(8,128)(2,1)}, u32[]{:S(2)}) copy-start(bf16[640,640]{1,0:T(8,128)(2,1)} %constant.51.clone) | copy-start | bytes 2457604
  0.1 10.8 %copy-start.4 = (s32[16,448]{1,0:T(8,128)S(1)}, s32[16,448]{1,0:T(8,128)}, u32[]{:S(2)}) copy-start(s32[16,448]{1,0:T(8,128)} %refs_0_.1) | copy-start | bytes 86020
  0.1 10.8 %copy-start.7 = (s32[16,448]{1,0:T(8,128)S(1)}, s32[16,448]{1,0:T(8,128)}, u32[]{:S(2)}) copy-start(s32[16,448]{1,0:T(8,128)} %refs_3_.1) | copy-start | bytes 86020
  0.1 10.8 %copy-start.8 = (s32[16,448]{1,0:T(8,128)S(1)}, s32[16,448]{1,0:T(8,128)}, u32[]{:S(2)}) copy-start(s32[16,448]{1,0:T(8,128)} %refs_4_.1) | copy-start | bytes 86020
  0.1 10.8 %copy-start.9 = (s32[16,320]{1,0:T(8,128)S(1)}, s32[16,320]{1,0:T(8,128)}, u32[]{:S(2)}) copy-start(s32[16,320]{1,0:T(8,128)} %refs_1_.1) | copy-start | bytes 61444
  0.1 10.8 %copy-start.10 = (s32[16,320]{1,0:T(8,128)S(1)}, s32[16,320]{1,0:T(8,128)}, u32[]{:S(2)}) copy-start(s32[16,320]{1,0:T(8,128)} %refs_2_.1) | copy-start | bytes 61444
  17.5 51.8 %all-to-all-start.3 = ((bf16[4,4,96,640]{3,2,1,0:T(8,128)(2,1)}), bf16[4,4,96,640]{3,2,1,0:T(8,128)(2,1)}, u32[]{:S(2)}, u32[]{:S(2)}) async-start(bf16[4,4,96,640]{3,2,1,0:T(8,128)(2,1)} %get-tuple-element.79), calls=%async_computation.3 | async-start | bytes 3932160 | tf_op jit(solution)/shard_map/cond/branch_1_fun/all_to_all | solution.py:539
  69.3 134.9 %all-to-all-start.4 = ((bf16[4,12,96,640]{3,2,1,0:T(8,128)(2,1)}), bf16[4,12,96,640]{3,2,1,0:T(8,128)(2,1)}, u32[]{:S(2)}, u32[]{:S(2)}) async-start(bf16[4,12,96,640]{3,2,1,0:T(8,128)(2,1)} %pack_sampled.3), calls=%async_computation.4 | async-start | bytes 11796480 | tf_op jit(solution)/shard_map/cond/branch_1_fun/all_to_all | solution.py:539
  75.0 77.6 %collective-permute-start.8 = (bf16[2,4,336,640]{3,2,1,0:T(8,128)(2,1)}, bf16[2,4,336,640]{3,2,1,0:T(8,128)(2,1)S(1)}, u32[]{:S(2)}, u32[]{:S(2)}) collective-permute-start(bf16[2,4,336,640]{3,2,1,0:T(8,128)(2,1)} %get-tuple-element.103), channel_id=1, source_target_pairs={{0,2},{1,3},{2,0},{3,1},{4,6},{5,7},{6,4},{7,5},{8,10},{9,11},{10,... | collective-permute-start | bytes 10321928 | tf_op jit(solution)/shard_map/cond/branch_1_fun/ppermute | solution.py:531
  82.6 94.0 %copy-start.14 = (bf16[112,112]{1,0:T(8,128)(2,1)S(1)}, bf16[112,112]{1,0:T(8,128)(2,1)}, u32[]{:S(2)}) copy-start(bf16[112,112]{1,0:T(8,128)(2,1)} %constant.53.clone.1) | copy-start | bytes 75268 | tf_op jit(solution)/shard_map/cond
  82.6 92.6 %collective-permute-start.2 = (bf16[2,4,112,640]{3,2,1,0:T(8,128)(2,1)}, bf16[2,4,112,640]{3,2,1,0:T(8,128)(2,1)S(1)}, u32[]{:S(2)}, u32[]{:S(2)}) collective-permute-start(bf16[2,4,112,640]{3,2,1,0:T(8,128)(2,1)} %get-tuple-element.86), channel_id=1, source_target_pairs={{0,2},{1,3},{2,0},{3,1},{4,6},{5,7},{6,4},{7,5},{8,10},{9,11},{10,... | collective-permute-start | bytes 3440648 | tf_op jit(solution)/shard_map/cond/branch_1_fun/ppermute | solution.py:531
  83.1 98.3 %collective-permute-start.7 = (bf16[4,336,640]{2,1,0:T(8,128)(2,1)}, bf16[4,336,640]{2,1,0:T(8,128)(2,1)}, u32[]{:S(2)}, u32[]{:S(2)}) collective-permute-start(bf16[4,336,640]{2,1,0:T(8,128)(2,1)} %get-tuple-element.102), channel_id=1, source_target_pairs={{0,1},{1,0},{2,3},{3,2},{4,5},{5,4},{6,7},{7,6},{8,9},{9,8},{10,11... | collective-permute-start | bytes 5160968 | tf_op jit(solution)/shard_map/cond/branch_1_fun/ppermute | solution.py:531
  152.6 23.6 %copy-start.3 = (bf16[2,4,336,640]{3,2,1,0:T(8,128)(2,1)}, bf16[2,4,336,640]{3,2,1,0:T(8,128)(2,1)S(1)}, u32[]{:S(2)}) copy-start(bf16[2,4,336,640]{3,2,1,0:T(8,128)(2,1)S(1)} %collective-permute-done.8.refs_2_) | copy-start | bytes 10321924 | tf_op jit(solution)/shard_map/cond
  154.1 27.3 %collective-permute-start.9 = (bf16[4,336,640]{2,1,0:T(8,128)(2,1)}, bf16[4,336,640]{2,1,0:T(8,128)(2,1)}, u32[]{:S(2)}, u32[]{:S(2)}) collective-permute-start(bf16[4,336,640]{2,1,0:T(8,128)(2,1)} %slice_bitcast_fusion.1), channel_id=1, source_target_pairs={{0,1},{1,0},{2,3},{3,2},{4,5},{5,4},{6,7},{7,6},{8,9},{9,8},{10,11... | collective-permute-start | bytes 5160968 | tf_op jit(solution)/shard_map/cond/branch_1_fun/ppermute | solution.py:531
  154.1 27.3 %collective-permute-start.1 = (bf16[4,112,640]{2,1,0:T(8,128)(2,1)}, bf16[4,112,640]{2,1,0:T(8,128)(2,1)}, u32[]{:S(2)}, u32[]{:S(2)}) collective-permute-start(bf16[4,112,640]{2,1,0:T(8,128)(2,1)} %get-tuple-element.85), channel_id=1, source_target_pairs={{0,1},{1,0},{2,3},{3,2},{4,5},{5,4},{6,7},{7,6},{8,9},{9,8},{10,11... | collective-permute-start | bytes 1720328 | tf_op jit(solution)/shard_map/cond/branch_1_fun/ppermute | solution.py:531
  175.2 1.3 copy-start.6
  176.2 5.2 %collective-permute-start.3 = (bf16[4,112,640]{2,1,0:T(8,128)(2,1)}, bf16[4,112,640]{2,1,0:T(8,128)(2,1)}, u32[]{:S(2)}, u32[]{:S(2)}) collective-permute-start(bf16[4,112,640]{2,1,0:T(8,128)(2,1)} %slice_bitcast_fusion.3), channel_id=1, source_target_pairs={{0,1},{1,0},{2,3},{3,2},{4,5},{5,4},{6,7},{7,6},{8,9},{9,8},{10,11... | collective-permute-start | bytes 1720328 | tf_op jit(solution)/shard_map/cond/branch_1_fun/ppermute | solution.py:531
  176.7 0.9 copy-start.13
  204.2 134.6 %all-to-all-start.5 = ((bf16[4,12,96,640]{3,2,1,0:T(8,128)(2,1)}), bf16[4,12,96,640]{3,2,1,0:T(8,128)(2,1)}, u32[]{:S(2)}, u32[]{:S(2)}) async-start(bf16[4,12,96,640]{3,2,1,0:T(8,128)(2,1)} %pack_sampled.5), calls=%async_computation.5 | async-start | bytes 11796480 | tf_op jit(solution)/shard_map/cond/branch_1_fun/all_to_all | solution.py:539
  220.3 77.6 %collective-permute-start.11 = (bf16[2,4,336,640]{3,2,1,0:T(8,128)(2,1)}, bf16[2,4,336,640]{3,2,1,0:T(8,128)(2,1)S(1)}, u32[]{:S(2)}, u32[]{:S(2)}) collective-permute-start(bf16[2,4,336,640]{3,2,1,0:T(8,128)(2,1)} %get-tuple-element.108), channel_id=1, source_target_pairs={{0,2},{1,3},{2,0},{3,1},{4,6},{5,7},{6,4},{7,5},{8,10},{9,11},{10,... | collective-permute-start | bytes 10321928 | tf_op jit(solution)/shard_map/cond/branch_1_fun/ppermute | solution.py:531
  240.6 58.8 %copy-start.15 = (bf16[4,112,640]{2,1,0:T(8,128)(2,1)S(1)}, bf16[4,112,640]{2,1,0:T(8,128)(2,1)}, u32[]{:S(2)}) copy-start(bf16[4,112,640]{2,1,0:T(8,128)(2,1)} %get-tuple-element.97) | copy-start | bytes 1720324 | tf_op jit(solution)/shard_map/cond
  240.6 79.9 %collective-permute-start.5 = (bf16[2,4,112,640]{3,2,1,0:T(8,128)(2,1)}, bf16[2,4,112,640]{3,2,1,0:T(8,128)(2,1)S(1)}, u32[]{:S(2)}, u32[]{:S(2)}) collective-permute-start(bf16[2,4,112,640]{3,2,1,0:T(8,128)(2,1)} %get-tuple-element.98), channel_id=1, source_target_pairs={{0,2},{1,3},{2,0},{3,1},{4,6},{5,7},{6,4},{7,5},{8,10},{9,11},{10,... | collective-permute-start | bytes 3440648 | tf_op jit(solution)/shard_map/cond/branch_1_fun/ppermute | solution.py:531
  241.1 86.8 %collective-permute-start.10 = (bf16[4,336,640]{2,1,0:T(8,128)(2,1)}, bf16[4,336,640]{2,1,0:T(8,128)(2,1)}, u32[]{:S(2)}, u32[]{:S(2)}) collective-permute-start(bf16[4,336,640]{2,1,0:T(8,128)(2,1)} %get-tuple-element.107), channel_id=1, source_target_pairs={{0,1},{1,0},{2,3},{3,2},{4,5},{5,4},{6,7},{7,6},{8,9},{9,8},{10,11... | collective-permute-start | bytes 5160968 | tf_op jit(solution)/shard_map/cond/branch_1_fun/ppermute | solution.py:531
  297.9 22.7 %copy-start.2 = (bf16[2,4,336,640]{3,2,1,0:T(8,128)(2,1)}, bf16[2,4,336,640]{3,2,1,0:T(8,128)(2,1)S(1)}, u32[]{:S(2)}) copy-start(bf16[2,4,336,640]{3,2,1,0:T(8,128)(2,1)S(1)} %collective-permute-done.11.refs_2_) | copy-start | bytes 10321924 | tf_op jit(solution)/shard_map/cond
  299.4 28.6 %collective-permute-start.12 = (bf16[4,336,640]{2,1,0:T(8,128)(2,1)}, bf16[4,336,640]{2,1,0:T(8,128)(2,1)}, u32[]{:S(2)}, u32[]{:S(2)}) collective-permute-start(bf16[4,336,640]{2,1,0:T(8,128)(2,1)} %slice_bitcast_fusion), channel_id=1, source_target_pairs={{0,1},{1,0},{2,3},{3,2},{4,5},{5,4},{6,7},{7,6},{8,9},{9,8},{10,11... | collective-permute-start | bytes 5160968 | tf_op jit(solution)/shard_map/cond/branch_1_fun/ppermute | solution.py:531
  299.4 21.3 %collective-permute-start.4 = (bf16[4,112,640]{2,1,0:T(8,128)(2,1)S(1)}, bf16[4,112,640]{2,1,0:T(8,128)(2,1)S(1)}, u32[]{:S(2)}, u32[]{:S(2)}) collective-permute-start(bf16[4,112,640]{2,1,0:T(8,128)(2,1)S(1)} %copy-done.15), channel_id=1, source_target_pairs={{0,1},{1,0},{2,3},{3,2},{4,5},{5,4},{6,7},{7,6},{8,9},{9,8},{10,11... | collective-permute-start | bytes 1720328 | tf_op jit(solution)/shard_map/cond/branch_1_fun/ppermute | solution.py:531
  320.5 2.2 copy-start.5
  320.6 2.2 collective-permute-start.6
  320.7 2.1 copy-start.12
  338.8 49.4 %all-to-all-start.6 = ((bf16[4,4,96,640]{3,2,1,0:T(8,128)(2,1)}), bf16[4,4,96,640]{3,2,1,0:T(8,128)(2,1)}, u32[]{:S(2)}, u32[]{:S(2)}) async-start(bf16[4,4,96,640]{3,2,1,0:T(8,128)(2,1)} %pack_sampled.4), calls=%async_computation.6 | async-start | bytes 3932160 | tf_op jit(solution)/shard_map/cond/branch_1_fun/all_to_all | solution.py:539
  398.1 8.9 %collective-permute-start.13 = (bf16[2,320,224]{2,1,0:T(8,128)(2,1)}, bf16[2,320,224]{2,1,0:T(8,128)(2,1)S(1)}, u32[]{:S(2)}, u32[]{:S(2)}) collective-permute-start(bf16[2,320,224]{2,1,0:T(8,128)(2,1)} %get-tuple-element.119), channel_id=1, source_target_pairs={{0,16},{16,0},{1,17},{17,1},{2,18},{18,2},{3,19},{19,3},{4,20},{20... | collective-permute-start | bytes 860168 | tf_op jit(solution)/shard_map/cond/branch_1_fun/ppermute | solution.py:546
  (1 other events, 0.8 us)
